TPU v7x, 32 devices: a whole 2x2x4 slice. The times are simulated.
32 devices in a mesh: sec: 4 (over y, x), tile: 4 (over z), half: 2 (over core).
Axes of the slice: x: 2, y: 2, z: 4, core: 2. Of those that a mesh axis runs over, the one named last changes fastest.
Arguments:
- sections_in: bfloat16 [8, 256, 1024], P('sec', 'tile', 'half'), parts along dimension 2, may hold values from -30 to 30
- first_kernel: bfloat16 [12, 1, 3, 3, 3], replicated, may hold values from -1.25 to 1.25
- first_bias: float32 [12], replicated, may hold values from -3 to 3
- second_kernel: bfloat16 [12, 12, 3, 3, 3], replicated, may hold values from -0.3125 to 0.3125
- second_bias: float32 [12], replicated, may hold values from -3 to 3
- head_kernel: bfloat16 [3, 12], replicated, may hold values from -1.75 to 1.75
- head_bias: float32 [3], replicated, may hold values from -3 to 3
Outputs:
- affinity: float32 [3, 8, 256, 1024], P(None, None, 'sec', ('half', 'tile')), parts along dimension 3
There are 2 independent parts, one for each index of `half`. A program takes and returns all parts, laid end to end along the dimension named above; an argument that names none is the same for every part. Nothing has to cross between parts.
All inputs are finite; a program needn't handle non-finite values.
Results may differ from a plain program's by a relative error of at most 0.0016.
Values may be sent and summed in bfloat16 or wider, within the bound.
A program may use at most 128 MiB of HBM per device.

v0:
```python
import jax
import jax.numpy as jnp
from jax import lax
from jax.sharding import PartitionSpec as P


def padded_2(shard, sides, width):
    for axis, dim in sides:
        peers, length = (lax.axis_size(axis), shard.shape[dim])
        up = [(i, (i + 1) % peers) for i in range(peers - 1)]
        down = [(j, i) for i, j in up]
        last = lax.slice_in_dim(shard, length - width, length, axis=dim)
        initial = lax.slice_in_dim(shard, 0, width, axis=dim)
        before = lax.ppermute(last, axis, up)
        after = lax.ppermute(initial, axis, down)
        shard = jnp.concatenate([before, shard, after], axis=dim)
    return shard


def convolve(volume, kernel, padding):
    return lax.conv_general_dilated(
        volume,
        kernel,
        (1, 1, 1),
        padding,
        dimension_numbers=("NCDHW", "OIDHW", "NCDHW"),
        preferred_element_type=jnp.float32,
    )


def activate(summed, bias):
    return jax.nn.relu(summed + bias[None, :, None, None, None]).astype(jnp.bfloat16)


def local_sums(volume):
    values = volume.astype(jnp.float32)
    return (jnp.sum(values, axis=(1, 2)), jnp.sum(values * values, axis=(1, 2)))


def normalize(volume, first_sum, second_sum, cells_total):
    average = first_sum / cells_total
    variance = second_sum / cells_total - average * average
    inv_std = lax.rsqrt(variance + 1e-05)
    shifted = volume.astype(jnp.float32) - average[:, None, None]
    return (shifted * inv_std[:, None, None]).astype(jnp.bfloat16)


def brick_normalize(volume):
    plain_sum, square_sum = local_sums(volume)
    first_sum, second_sum = lax.psum((plain_sum, square_sum), ("sec", "tile"))
    cells_total = volume.shape[1] * volume.shape[2] * lax.axis_size("sec") * lax.axis_size("tile")
    return normalize(volume, first_sum, second_sum, cells_total)


def regroup(volume):
    return lax.all_to_all(
        lax.all_to_all(volume, "tile", split_axis=2, concat_axis=1, tiled=True),
        "sec",
        split_axis=1,
        concat_axis=0,
        tiled=True,
    )


def finish(widened, second_kernel, second_bias, head_kernel, head_bias):
    second_out = activate(
        convolve(widened[None], second_kernel, ((1, 1), (0, 0), (0, 0))), second_bias
    )
    logits = jnp.einsum(
        "oc,czyx->ozyx", head_kernel, second_out[0], preferred_element_type=jnp.float32
    )
    return jax.nn.sigmoid(logits + head_bias[:, None, None, None])


def per_device(
    sections_in, first_kernel, first_bias, second_kernel, second_bias, head_kernel, head_bias
):
    level = ((1, 1), (0, 0), (0, 0))
    brick = brick_normalize(regroup(sections_in))
    padded = padded_2(brick, (("sec", 1), ("tile", 2)), 2)
    first_out = activate(convolve(padded[None, None], first_kernel, level), first_bias)[0]
    rows_here = brick.shape[1]
    cols_here = brick.shape[2]
    row_index = lax.axis_index("sec") * rows_here - 1 + jnp.arange(rows_here + 2, dtype=jnp.int32)
    col_index = lax.axis_index("tile") * cols_here - 1 + jnp.arange(cols_here + 2, dtype=jnp.int32)
    row_inside = (row_index >= 0) & (row_index < rows_here * lax.axis_size("sec"))
    col_inside = (col_index >= 0) & (col_index < cols_here * lax.axis_size("tile"))
    inside = row_inside[:, None] & col_inside[None, :]
    widened = jnp.where(inside[None, None], first_out, jnp.zeros((), jnp.bfloat16))
    return finish(widened, second_kernel, second_bias, head_kernel, head_bias)


def solution(mesh):
    in_specs = (P("sec", "tile", "half"), P(), P(), P(), P(), P(), P())
    out_specs = P(None, None, "sec", ("half", "tile"))
    return jax.shard_map(
        per_device, mesh=mesh, in_specs=in_specs, out_specs=out_specs, check_vma=False
    )
```

profile of v0, /device:TPU:0, one launch (start us, length us, event | category | flops | bytes accessed | tf_op | source)
XLA Modules:
  0.0 273.2 jit_solution(5084673572646575382)
XLA Ops:
  0.0 1.1 copy.95
  1.1 0.9 reshape.84
  2.0 6.3 %all-to-all-start = ((bf16[4,2,8192]{2,1,0:T(2,128)(2,1)}), bf16[4,2,8192]{2,1,0:T(2,128)(2,1)S(1)}, u32[]{:S(2)}, u32[]{:S(2)}) async-start(bf16[4,2,8192]{2,1,0:T(2,128)(2,1)} %reshape.84), calls=%async_computation | async-start | bytes 262144 | tf_op jit(solution)/shard_map/all_to_all | solution.py:57
  8.3 6.1 %all-to-all-done = bf16[4,2,8192]{2,1,0:T(2,128)(2,1)S(1)} async-done(((bf16[4,2,8192]{2,1,0:T(2,128)(2,1)}), bf16[4,2,8192]{2,1,0:T(2,128)(2,1)S(1)}, u32[]{:S(2)}, u32[]{:S(2)}) %all-to-all-start) | async-done | bytes 131104 | tf_op jit(solution)/shard_map/all_to_all | solution.py:57
  15.6 3.7 %all-to-all-start.1 = ((bf16[2,256,128]{2,0,1:T(2,128)(2,1)}), bf16[2,256,128]{2,0,1:T(2,128)(2,1)S(1)}, u32[]{:S(2)}, u32[]{:S(2)}) async-start(bf16[2,256,128]{2,0,1:T(2,128)(2,1)} %copy.98), calls=%async_computation.1 | async-start | bytes 262144 | tf_op jit(solution)/shard_map/all_to_all | solution.py:56
  19.3 5.0 %all-to-all-done.1 = bf16[2,256,128]{2,0,1:T(2,128)(2,1)S(1)} async-done(((bf16[2,256,128]{2,0,1:T(2,128)(2,1)}), bf16[2,256,128]{2,0,1:T(2,128)(2,1)S(1)}, u32[]{:S(2)}, u32[]{:S(2)}) %all-to-all-start.1) | async-done | bytes 131104 | tf_op jit(solution)/shard_map/all_to_all | solution.py:56
  24.9 38.3 %all-reduce = (f32[8]{0:T(128)S(1)}, f32[8]{0:T(128)S(1)}) all-reduce(f32[8]{0:T(128)S(1)} %reduce_sum.25, f32[8]{0:T(128)S(1)} %reduce_sum.23), channel_id=1, replica_groups=mesh['sec'=4,'tile'=4,'half'=2] {'sec','tile'}, use_global_device_ids=true, to_apply=%region_3.0 | all-reduce | flops 16 | bytes 128 | tf_op jit(solution)/shard_map/psum | solution.py:50
  63.4 1.3 collective-permute-start
  64.7 1.3 collective-permute-start.1
  66.0 5.9 %collective-permute-done.1 = bf16[8,2,128]{2,1,0:T(2,128)(2,1)S(1)} collective-permute-done((bf16[8,2,128]{2,1,0:T(2,128)(2,1)S(1)}, bf16[8,2,128]{2,1,0:T(2,128)(2,1)S(1)}, u32[]{:S(2)}, u32[]{:S(2)}) %collective-permute-start.1) | collective-permute-done | bytes 4128 | tf_op jit(solution)/shard_map/ppermute | solution.py:15
  72.1 1.6 collective-permute-start.2
  73.7 1.3 collective-permute-start.3
  75.1 1.3 collective-permute-done.2
  76.4 4.4 %collective-permute-done.3 = bf16[8,68,2]{2,1,0:T(8,128)(2,1)S(1)} collective-permute-done((bf16[8,68,2]{2,1,0:T(8,128)(2,1)S(1)}, bf16[8,68,2]{2,1,0:T(8,128)(2,1)S(1)}, u32[]{:S(2)}, u32[]{:S(2)}) %collective-permute-start.3) | collective-permute-done | bytes 2208 | tf_op jit(solution)/shard_map/ppermute | solution.py:15
  81.4 10.0 %copy.105 = bf16[1,8,68,8,19]{3,0,4,2,1:T(2,128)(2,1)} copy(bf16[1,8,68,8,19]{2,1,4,3,0:T(8,128)(2,1)S(1)} %fusion.34) | data formatting | bytes 330752 | tf_op jit(solution)/shard_map/conv_general_dilated | solution.py:21
  91.4 62.1 %maximum_convert_fusion = bf16[8,66,8,17,12]{4,2,3,1,0:T(8,128)(2,1)} fusion(f32[12]{0:T(128)} %param.9, pred[8,17]{0,1:T(8,128)(4,1)} %constant.50, bf16[1,8,68,8,19]{3,0,4,2,1:T(2,128)(2,1)} %copy.105, bf16[12,1,3,3,3]{0,4,3,2,1:T(4,128)(2,1)} %param.8), kind=kOutput, calls=%fused_computation.2 | convolution fusion | flops 46100736 | bytes 1889600 | tf_op jit(solution)/shard_map/conv_general_dilated | solution.py:21
  153.5 18.6 %copy.107 = bf16[8,66,8,17,12]{1,0,4,3,2:T(8,128)(2,1)S(1)} copy(bf16[8,66,8,17,12]{4,2,3,1,0:T(8,128)(2,1)} %maximum_convert_fusion) | data formatting | bytes 3446784 | tf_op jit(solution)/shard_map/convert_element_type | solution.py:32
  173.9 16.7 %copy.110 = bf16[12,8,66,1,8,17]{0,4,5,2,1,3:T(8,128)(2,1)} copy(bf16[12,8,66,1,8,17]{2,1,5,4,0,3:T(8,128)(2,1)S(1)} %bitcast.62) | data formatting | bytes 3446784 | tf_op jit(solution)/shard_map/conv_general_dilated | solution.py:21
  190.5 2.2 slice.26
  192.8 50.5 %maximum_convert_fusion.1 = bf16[8,64,8,17,12]{4,2,3,1,0:T(8,128)(2,1)} fusion(f32[12]{0:T(128)S(1)} %copy-done.2, pred[8,17]{0,1:T(8,128)(4,1)S(1)} %copy-done.4, bf16[12,8,66,1,7,2]{0,4,5,2,1,3:T(8,128)(2,1)S(1)} %slice.26, bf16[12,8,66,1,8,17]{0,4,5,2,1,3:T(8,128)(2,1)} %copy.110, bf16[12,12,3,3,3]{1,4,3,2,0:T(4,128)(2,1)S(1)} %copy-done), kind=kOutput, calls=%fused_computation.3 | convolution fusion | flops 505457664 | bytes 3579928 | tf_op jit(solution)/shard_map/conv_general_dilated | solution.py:21
  243.3 18.9 %copy.112 = bf16[8,64,8,17,12]{1,0,4,3,2:T(8,128)(2,1)S(1)} copy(bf16[8,64,8,17,12]{4,2,3,1,0:T(8,128)(2,1)} %maximum_convert_fusion.1) | data formatting | bytes 3342336 | tf_op jit(solution)/shard_map/convert_element_type | solution.py:32
  262.2 1.8 slice.27
  264.0 7.5 %copy.119 = bf16[8,64,1,128,12]{3,4,1,0,2:T(8,128)(2,1)S(1)} copy(bf16[8,64,1,128,12]{1,0,4,3,2:T(8,128)(2,1)} %slice.27) | data formatting | bytes 3145728
  272.3 1.0 copy.114
  (39 shorter events, 5.2 us)
Async XLA Ops:
  0.0 192.7 %copy-start = (bf16[12,12,3,3,3]{1,4,3,2,0:T(4,128)(2,1)S(1)}, bf16[12,12,3,3,3]{1,4,3,2,0:T(4,128)(2,1)}, u32[]{:S(2)}) copy-start(bf16[12,12,3,3,3]{1,4,3,2,0:T(4,128)(2,1)} %param.10) | copy-start | bytes 23332
  2.0 12.4 %all-to-all-start = ((bf16[4,2,8192]{2,1,0:T(2,128)(2,1)}), bf16[4,2,8192]{2,1,0:T(2,128)(2,1)S(1)}, u32[]{:S(2)}, u32[]{:S(2)}) async-start(bf16[4,2,8192]{2,1,0:T(2,128)(2,1)} %reshape.84), calls=%async_computation | async-start | bytes 262144 | tf_op jit(solution)/shard_map/all_to_all | solution.py:57
  15.6 8.7 %all-to-all-start.1 = ((bf16[2,256,128]{2,0,1:T(2,128)(2,1)}), bf16[2,256,128]{2,0,1:T(2,128)(2,1)S(1)}, u32[]{:S(2)}, u32[]{:S(2)}) async-start(bf16[2,256,128]{2,0,1:T(2,128)(2,1)} %copy.98), calls=%async_computation.1 | async-start | bytes 262144 | tf_op jit(solution)/shard_map/all_to_all | solution.py:56
  63.4 2.6 collective-permute-start
  64.7 7.2 %collective-permute-start.1 = (bf16[8,2,128]{2,1,0:T(2,128)(2,1)S(1)}, bf16[8,2,128]{2,1,0:T(2,128)(2,1)S(1)}, u32[]{:S(2)}, u32[]{:S(2)}) collective-permute-start(bf16[8,2,128]{2,1,0:T(2,128)(2,1)S(1)} %get-tuple-element.12), channel_id=1, source_target_pairs={{8,0},{16,8},{24,16},{9,1},{17,9},{25,17},{10,2},{18,10},{26,18},{... | collective-permute-start | bytes 12296 | tf_op jit(solution)/shard_map/ppermute | solution.py:15
  72.1 4.2 %collective-permute-start.2 = (bf16[8,68,2]{2,1,0:T(8,128)(2,1)S(1)}, bf16[8,68,2]{2,1,0:T(8,128)(2,1)S(1)}, u32[]{:S(2)}, u32[]{:S(2)}) collective-permute-start(bf16[8,68,2]{2,1,0:T(8,128)(2,1)S(1)} %get-tuple-element.9), channel_id=1, source_target_pairs={{0,2},{2,4},{4,6},{1,3},{3,5},{5,7},{8,10},{10,12},{12,14},{9,11},... | collective-permute-start | bytes 6536 | tf_op jit(solution)/shard_map/ppermute | solution.py:14
  73.7 7.0 %collective-permute-start.3 = (bf16[8,68,2]{2,1,0:T(8,128)(2,1)S(1)}, bf16[8,68,2]{2,1,0:T(8,128)(2,1)S(1)}, u32[]{:S(2)}, u32[]{:S(2)}) collective-permute-start(bf16[8,68,2]{2,1,0:T(8,128)(2,1)S(1)} %get-tuple-element.10), channel_id=1, source_target_pairs={{2,0},{4,2},{6,4},{3,1},{5,3},{7,5},{10,8},{12,10},{14,12},{11,9},... | collective-permute-start | bytes 6536 | tf_op jit(solution)/shard_map/ppermute | solution.py:15
  172.4 20.3 %copy-start.2 = (f32[12]{0:T(128)S(1)}, f32[12]{0:T(128)}, u32[]{:S(2)}) copy-start(f32[12]{0:T(128)} %param.11) | copy-start | bytes 148
  172.5 20.3 %copy-start.4 = (pred[8,17]{0,1:T(8,128)(4,1)S(1)}, pred[8,17]{0,1:T(8,128)(4,1)}, u32[]{:S(2)}) copy-start(pred[8,17]{0,1:T(8,128)(4,1)} %constant.49) | copy-start | bytes 412
  243.3 28.2 %copy-start.1 = (bf16[3,12]{1,0:T(4,128)(2,1)S(1)}, bf16[3,12]{1,0:T(4,128)(2,1)}, u32[]{:S(2)}) copy-start(bf16[3,12]{1,0:T(4,128)(2,1)} %param.12) | copy-start | bytes 220
  243.3 28.2 %copy-start.3 = (f32[3]{0:T(128)S(1)}, f32[3]{0:T(128)}, u32[]{:S(2)}) copy-start(f32[3]{0:T(128)} %param.13) | copy-start | bytes 40
where the time goes:
time: 274 us; the launch traced here: 273 us
  matrix products  113 us (41%)
  local copies, waits for them, and re-layouts  82.1 us (30%)
  blocking collectives  38.3 us (14%)
  waiting for transfers between devices  22.7 us (8%)
  starting transfers between devices  15.5 us (6%)
    conv_general_dilated x2, matrix products, convolve(): lax.conv_general_dilated(volume, kernel, (1, 1, 1), padding, dimension_nu...  113 us
    convert_element_type x3, local copies, waits for them, and re-layouts, activate(): jax.nn.relu(summed + bias[None, :, None, None, None]).astype(jnp.bfloat16)  39.4 us
    psum x1, blocking collectives, brick_normalize(): first_sum, second_sum = lax.psum((plain_sum, square_sum), ('sec', 'tile'))  38.3 us
    conv_general_dilated x4, local copies, waits for them, and re-layouts, convolve(): lax.conv_general_dilated(volume, kernel, (1, 1, 1), padding, dimension_nu...  28.8 us
    unnamed x16, local copies, waits for them, and re-layouts  10.6 us
    ppermute x2, waiting for transfers between devices, padded_2(): after = lax.ppermute(initial, axis, down)  10.3 us
    all_to_all x1, starting transfers between devices, regroup(): lax.all_to_all(volume, 'tile', split_axis=2, concat_axis=1, tiled=True)  6.32 us
    all_to_all x1, waiting for transfers between devices, regroup(): lax.all_to_all(volume, 'tile', split_axis=2, concat_axis=1, tiled=True)  6.07 us
  transfers between devices with their start and end apart: 6, of which 5 were waited for; matrix products, arithmetic and copies ran while one was open for 0% of the time, Pallas kernels for 0%

commit v1 on v0

--- a/solution.py
+++ b/solution.py
@@ -47,7 +47,15 @@
 
 def brick_normalize(volume):
     plain_sum, square_sum = local_sums(volume)
-    first_sum, second_sum = lax.psum((plain_sum, square_sum), ("sec", "tile"))
+
+    def review_links(unit):
+        along_axis = "sec"
+        bus_axis = "tile"
+        for no in (bus_axis, along_axis):
+            unit = lax.psum(unit, no)
+        return unit
+
+    first_sum, second_sum = review_links((plain_sum, square_sum))
     cells_total = volume.shape[1] * volume.shape[2] * lax.axis_size("sec") * lax.axis_size("tile")
     return normalize(volume, first_sum, second_sum, cells_total)
 

time: 274 us -> 255 us (0.931)
  blocking collectives: 38.3 us -> 18.2 us
    psum x1 -> x2, blocking collectives: 38.3 us -> 18.2 us  [review_links(): unit = lax.psum(unit, no)]
where the time goes in v1:
time: 255 us; the launch traced here: 254 us
  matrix products  113 us (44%)
  local copies, waits for them, and re-layouts  82.2 us (32%)
  waiting for transfers between devices  20.9 us (8%)
  blocking collectives  18.2 us (7%)
  starting transfers between devices  18 us (7%)
    conv_general_dilated x2, matrix products, convolve(): lax.conv_general_dilated(volume, kernel, (1, 1, 1), padding, dimension_nu...  113 us
    convert_element_type x3, local copies, waits for them, and re-layouts, activate(): jax.nn.relu(summed + bias[None, :, None, None, None]).astype(jnp.bfloat16)  39.4 us
    conv_general_dilated x4, local copies, waits for them, and re-layouts, convolve(): lax.conv_general_dilated(volume, kernel, (1, 1, 1), padding, dimension_nu...  28.9 us
    psum x2, blocking collectives, review_links(): unit = lax.psum(unit, no)  18.2 us
    unnamed x16, local copies, waits for them, and re-layouts  10.6 us
    ppermute x2, waiting for transfers between devices, padded_2(): after = lax.ppermute(initial, axis, down)  8.56 us
    all_to_all x1, starting transfers between devices, regroup(): lax.all_to_all(volume, 'tile', split_axis=2, concat_axis=1, tiled=True)  6.32 us
    all_to_all x1, waiting for transfers between devices, regroup(): lax.all_to_all(volume, 'tile', split_axis=2, concat_axis=1, tiled=True)  6.07 us
  transfers between devices with their start and end apart: 6, of which 5 were waited for; matrix products, arithmetic and copies ran while one was open for 0% of the time, Pallas kernels for 0%

profile of v1, /device:TPU:0, one launch (start us, length us, event | category | flops | bytes accessed | tf_op | source)
XLA Modules:
  0.0 253.9 jit_solution(1500928475265500777)
XLA Ops:
  0.0 1.1 copy.95
  2.0 6.3 %all-to-all-start = ((bf16[4,2,8192]{2,1,0:T(2,128)(2,1)}), bf16[4,2,8192]{2,1,0:T(2,128)(2,1)S(1)}, u32[]{:S(2)}, u32[]{:S(2)}) async-start(bf16[4,2,8192]{2,1,0:T(2,128)(2,1)} %reshape.84), calls=%async_computation | async-start | bytes 262144 | tf_op jit(solution)/shard_map/all_to_all | solution.py:65
  8.3 6.1 %all-to-all-done = bf16[4,2,8192]{2,1,0:T(2,128)(2,1)S(1)} async-done(((bf16[4,2,8192]{2,1,0:T(2,128)(2,1)}), bf16[4,2,8192]{2,1,0:T(2,128)(2,1)S(1)}, u32[]{:S(2)}, u32[]{:S(2)}) %all-to-all-start) | async-done | bytes 131104 | tf_op jit(solution)/shard_map/all_to_all | solution.py:65
  15.6 3.7 %all-to-all-start.1 = ((bf16[2,256,128]{2,0,1:T(2,128)(2,1)}), bf16[2,256,128]{2,0,1:T(2,128)(2,1)S(1)}, u32[]{:S(2)}, u32[]{:S(2)}) async-start(bf16[2,256,128]{2,0,1:T(2,128)(2,1)} %copy.98), calls=%async_computation.1 | async-start | bytes 262144 | tf_op jit(solution)/shard_map/all_to_all | solution.py:64
  19.3 5.0 %all-to-all-done.1 = bf16[2,256,128]{2,0,1:T(2,128)(2,1)S(1)} async-done(((bf16[2,256,128]{2,0,1:T(2,128)(2,1)}), bf16[2,256,128]{2,0,1:T(2,128)(2,1)S(1)}, u32[]{:S(2)}, u32[]{:S(2)}) %all-to-all-start.1) | async-done | bytes 131104 | tf_op jit(solution)/shard_map/all_to_all | solution.py:64
  24.9 9.8 %all-reduce = (f32[8]{0:T(128)S(1)}, f32[8]{0:T(128)S(1)}) all-reduce(f32[8]{0:T(128)S(1)} %reduce_sum.25, f32[8]{0:T(128)S(1)} %reduce_sum.23), channel_id=1, replica_groups=mesh['sec'=4,'tile'=4,'half'=2] {'tile'}, use_global_device_ids=true, to_apply=%region_4.0 | all-reduce | flops 16 | bytes 128 | tf_op jit(solution)/shard_map/psum | solution.py:55
  34.8 8.4 %all-reduce.1 = (f32[8]{0:T(128)S(1)}, f32[8]{0:T(128)S(1)}) all-reduce(f32[8]{0:T(128)S(1)} %get-tuple-element.7, f32[8]{0:T(128)S(1)} %get-tuple-element.8), channel_id=1, replica_groups=mesh['sec'=4,'tile'=4,'half'=2] {'sec'}, use_global_device_ids=true, to_apply=%region_5.0 | all-reduce | flops 16 | bytes 128 | tf_op jit(solution)/shard_map/psum | solution.py:55
  43.3 3.0 %collective-permute-start = (bf16[8,2,128]{2,1,0:T(2,128)(2,1)S(1)}, bf16[8,2,128]{2,1,0:T(2,128)(2,1)S(1)}, u32[]{:S(2)}, u32[]{:S(2)}) collective-permute-start(bf16[8,2,128]{2,1,0:T(2,128)(2,1)S(1)} %get-tuple-element.13), channel_id=1, source_target_pairs={{0,8},{8,16},{16,24},{1,9},{9,17},{17,25},{2,10},{10,18},{18,26},{... | collective-permute-start | bytes 12296 | tf_op jit(solution)/shard_map/ppermute | solution.py:14
  46.2 1.3 collective-permute-start.1
  47.6 4.2 %collective-permute-done.1 = bf16[8,2,128]{2,1,0:T(2,128)(2,1)S(1)} collective-permute-done((bf16[8,2,128]{2,1,0:T(2,128)(2,1)S(1)}, bf16[8,2,128]{2,1,0:T(2,128)(2,1)S(1)}, u32[]{:S(2)}, u32[]{:S(2)}) %collective-permute-start.1) | collective-permute-done | bytes 4128 | tf_op jit(solution)/shard_map/ppermute | solution.py:15
  51.9 2.4 collective-permute-start.2
  54.3 1.3 collective-permute-start.3
  55.7 1.3 collective-permute-done.2
  57.0 4.4 %collective-permute-done.3 = bf16[8,68,2]{2,1,0:T(8,128)(2,1)S(1)} collective-permute-done((bf16[8,68,2]{2,1,0:T(8,128)(2,1)S(1)}, bf16[8,68,2]{2,1,0:T(8,128)(2,1)S(1)}, u32[]{:S(2)}, u32[]{:S(2)}) %collective-permute-start.3) | collective-permute-done | bytes 2208 | tf_op jit(solution)/shard_map/ppermute | solution.py:15
  62.1 10.1 %copy.105 = bf16[1,8,68,8,19]{3,0,4,2,1:T(2,128)(2,1)} copy(bf16[1,8,68,8,19]{2,1,4,3,0:T(8,128)(2,1)S(1)} %fusion.34) | data formatting | bytes 330752 | tf_op jit(solution)/shard_map/conv_general_dilated | solution.py:21
  72.2 62.1 %maximum_convert_fusion = bf16[8,66,8,17,12]{4,2,3,1,0:T(8,128)(2,1)} fusion(f32[12]{0:T(128)} %param.9, pred[8,17]{0,1:T(8,128)(4,1)} %constant.50, bf16[1,8,68,8,19]{3,0,4,2,1:T(2,128)(2,1)} %copy.105, bf16[12,1,3,3,3]{0,4,3,2,1:T(4,128)(2,1)} %param.8), kind=kOutput, calls=%fused_computation.2 | convolution fusion | flops 46100736 | bytes 1889600 | tf_op jit(solution)/shard_map/conv_general_dilated | solution.py:21
  134.2 18.6 %copy.107 = bf16[8,66,8,17,12]{1,0,4,3,2:T(8,128)(2,1)S(1)} copy(bf16[8,66,8,17,12]{4,2,3,1,0:T(8,128)(2,1)} %maximum_convert_fusion) | data formatting | bytes 3446784 | tf_op jit(solution)/shard_map/convert_element_type | solution.py:32
  154.6 16.7 %copy.110 = bf16[12,8,66,1,8,17]{0,4,5,2,1,3:T(8,128)(2,1)} copy(bf16[12,8,66,1,8,17]{2,1,5,4,0,3:T(8,128)(2,1)S(1)} %bitcast.62) | data formatting | bytes 3446784 | tf_op jit(solution)/shard_map/conv_general_dilated | solution.py:21
  171.3 2.2 slice.26
  173.5 50.5 %maximum_convert_fusion.1 = bf16[8,64,8,17,12]{4,2,3,1,0:T(8,128)(2,1)} fusion(f32[12]{0:T(128)S(1)} %copy-done.2, pred[8,17]{0,1:T(8,128)(4,1)S(1)} %copy-done.4, bf16[12,8,66,1,7,2]{0,4,5,2,1,3:T(8,128)(2,1)S(1)} %slice.26, bf16[12,8,66,1,8,17]{0,4,5,2,1,3:T(8,128)(2,1)} %copy.110, bf16[12,12,3,3,3]{1,4,3,2,0:T(4,128)(2,1)S(1)} %copy-done), kind=kOutput, calls=%fused_computation.3 | convolution fusion | flops 505457664 | bytes 3579928 | tf_op jit(solution)/shard_map/conv_general_dilated | solution.py:21
  224.0 18.9 %copy.112 = bf16[8,64,8,17,12]{1,0,4,3,2:T(8,128)(2,1)S(1)} copy(bf16[8,64,8,17,12]{4,2,3,1,0:T(8,128)(2,1)} %maximum_convert_fusion.1) | data formatting | bytes 3342336 | tf_op jit(solution)/shard_map/convert_element_type | solution.py:32
  242.9 1.8 slice.27
  244.7 7.5 %copy.119 = bf16[8,64,1,128,12]{3,4,1,0,2:T(8,128)(2,1)S(1)} copy(bf16[8,64,1,128,12]{1,0,4,3,2:T(8,128)(2,1)} %slice.27) | data formatting | bytes 3145728
  252.9 1.0 copy.114
  (40 shorter events, 6.1 us)
Async XLA Ops:
  0.0 173.5 %copy-start = (bf16[12,12,3,3,3]{1,4,3,2,0:T(4,128)(2,1)S(1)}, bf16[12,12,3,3,3]{1,4,3,2,0:T(4,128)(2,1)}, u32[]{:S(2)}) copy-start(bf16[12,12,3,3,3]{1,4,3,2,0:T(4,128)(2,1)} %param.10) | copy-start | bytes 23332
  2.0 12.4 %all-to-all-start = ((bf16[4,2,8192]{2,1,0:T(2,128)(2,1)}), bf16[4,2,8192]{2,1,0:T(2,128)(2,1)S(1)}, u32[]{:S(2)}, u32[]{:S(2)}) async-start(bf16[4,2,8192]{2,1,0:T(2,128)(2,1)} %reshape.84), calls=%async_computation | async-start | bytes 262144 | tf_op jit(solution)/shard_map/all_to_all | solution.py:65
  15.6 8.7 %all-to-all-start.1 = ((bf16[2,256,128]{2,0,1:T(2,128)(2,1)}), bf16[2,256,128]{2,0,1:T(2,128)(2,1)S(1)}, u32[]{:S(2)}, u32[]{:S(2)}) async-start(bf16[2,256,128]{2,0,1:T(2,128)(2,1)} %copy.98), calls=%async_computation.1 | async-start | bytes 262144 | tf_op jit(solution)/shard_map/all_to_all | solution.py:64
  43.3 4.3 %collective-permute-start = (bf16[8,2,128]{2,1,0:T(2,128)(2,1)S(1)}, bf16[8,2,128]{2,1,0:T(2,128)(2,1)S(1)}, u32[]{:S(2)}, u32[]{:S(2)}) collective-permute-start(bf16[8,2,128]{2,1,0:T(2,128)(2,1)S(1)} %get-tuple-element.13), channel_id=1, source_target_pairs={{0,8},{8,16},{16,24},{1,9},{9,17},{17,25},{2,10},{10,18},{18,26},{... | collective-permute-start | bytes 12296 | tf_op jit(solution)/shard_map/ppermute | solution.py:14
  46.2 5.5 %collective-permute-start.1 = (bf16[8,2,128]{2,1,0:T(2,128)(2,1)S(1)}, bf16[8,2,128]{2,1,0:T(2,128)(2,1)S(1)}, u32[]{:S(2)}, u32[]{:S(2)}) collective-permute-start(bf16[8,2,128]{2,1,0:T(2,128)(2,1)S(1)} %get-tuple-element.14), channel_id=1, source_target_pairs={{8,0},{16,8},{24,16},{9,1},{17,9},{25,17},{10,2},{18,10},{26,18},{... | collective-permute-start | bytes 12296 | tf_op jit(solution)/shard_map/ppermute | solution.py:15
  51.9 5.1 %collective-permute-start.2 = (bf16[8,68,2]{2,1,0:T(8,128)(2,1)S(1)}, bf16[8,68,2]{2,1,0:T(8,128)(2,1)S(1)}, u32[]{:S(2)}, u32[]{:S(2)}) collective-permute-start(bf16[8,68,2]{2,1,0:T(8,128)(2,1)S(1)} %get-tuple-element.11), channel_id=1, source_target_pairs={{0,2},{2,4},{4,6},{1,3},{3,5},{5,7},{8,10},{10,12},{12,14},{9,11},... | collective-permute-start | bytes 6536 | tf_op jit(solution)/shard_map/ppermute | solution.py:14
  54.3 7.0 %collective-permute-start.3 = (bf16[8,68,2]{2,1,0:T(8,128)(2,1)S(1)}, bf16[8,68,2]{2,1,0:T(8,128)(2,1)S(1)}, u32[]{:S(2)}, u32[]{:S(2)}) collective-permute-start(bf16[8,68,2]{2,1,0:T(8,128)(2,1)S(1)} %get-tuple-element.12), channel_id=1, source_target_pairs={{2,0},{4,2},{6,4},{3,1},{5,3},{7,5},{10,8},{12,10},{14,12},{11,9},... | collective-permute-start | bytes 6536 | tf_op jit(solution)/shard_map/ppermute | solution.py:15
  153.2 20.3 %copy-start.2 = (f32[12]{0:T(128)S(1)}, f32[12]{0:T(128)}, u32[]{:S(2)}) copy-start(f32[12]{0:T(128)} %param.11) | copy-start | bytes 148
  153.2 20.3 %copy-start.4 = (pred[8,17]{0,1:T(8,128)(4,1)S(1)}, pred[8,17]{0,1:T(8,128)(4,1)}, u32[]{:S(2)}) copy-start(pred[8,17]{0,1:T(8,128)(4,1)} %constant.49) | copy-start | bytes 412
  224.0 28.2 %copy-start.1 = (bf16[3,12]{1,0:T(4,128)(2,1)S(1)}, bf16[3,12]{1,0:T(4,128)(2,1)}, u32[]{:S(2)}) copy-start(bf16[3,12]{1,0:T(4,128)(2,1)} %param.12) | copy-start | bytes 220
  224.0 28.2 %copy-start.3 = (f32[3]{0:T(128)S(1)}, f32[3]{0:T(128)}, u32[]{:S(2)}) copy-start(f32[3]{0:T(128)} %param.13) | copy-start | bytes 40
